TPU v7x, 256 devices: a whole 4x4x8 slice. The times are simulated.
256 devices in a mesh: seq: 16 (over y, x), tensor: 16 (over z, core).
Axes of the slice: x: 4, y: 4, z: 8, core: 2. Of those that a mesh axis runs over, the one named last changes fastest.
Arguments:
- hidden_in: bfloat16 [1024, 8192], P('seq'), may hold values from -24 to 24
- gate_codes: bfloat16 [8192, 53248], P('seq', 'tensor'), may hold values from -8 to 7, as said below
- up_codes: bfloat16 [8192, 53248], P('seq', 'tensor'), may hold values from -8 to 7, as said below
- gate_scale: float32 [53248], P('tensor'), may hold values from 0.0015 to 0.006
- up_scale: float32 [53248], P('tensor'), may hold values from 0.0015 to 0.006
- down_codes: bfloat16 [53248, 8192], P('tensor', 'seq'), may hold values from -8 to 7, as said below
- down_scale: float32 [8192], P('seq'), may hold values from 0.0007 to 0.0028
- sign_bits: int32 [53248], P('tensor'), may hold values from 0 to 1
- had52: int32 [52, 52], replicated, may hold values from -1 to 1, as said below
Outputs:
- mixed: bfloat16 [1024, 8192], P('tensor', 'seq')
Inputs may be any that keep to these rules, and one draw needn't show every extreme that they name: `gate_codes`: every entry is a whole number. `up_codes`: every entry is a whole number. `down_codes`: every entry is a whole number. had52 is a Hadamard matrix: entries -1 or 1, rows mutually orthogonal.
All inputs are finite; a program needn't handle non-finite values.
Results may differ from a plain program's by a relative error of at most 0.024.
Values may be sent and summed in bfloat16 or wider, within the bound.
A program may use at most 192 MiB of HBM per device.

v0:
```python
import math

import jax
import jax.numpy as jnp
from jax import lax
from jax.sharding import PartitionSpec as P

FF = 53248


def partner_2(shard, axis, distance):
    return lax.ppermute(shard, axis, [(i, i ^ 1 << distance) for i in range(lax.axis_size(axis))])


def sylvester(length):
    indices = jnp.arange(length, dtype=jnp.int32)
    common_bits = jnp.bitwise_and(indices[:, None], indices[None, :])
    ones_count = jnp.zeros((length, length), jnp.int32)
    for shift_by in range(length.bit_length() - 1):
        ones_count = ones_count + jnp.bitwise_and(jnp.right_shift(common_bits, shift_by), 1)
    return (1 - 2 * (ones_count % 2)).astype(jnp.float32)


def per_device(
    hidden_in, gate_codes, up_codes, gate_scale, up_scale, down_codes, down_scale, sign_bits, had52
):
    values = hidden_in.astype(jnp.float32)
    normed = (values * lax.rsqrt(jnp.mean(values * values, axis=1, keepdims=True) + 1e-05)).astype(
        jnp.bfloat16
    )
    columns = lax.all_to_all(normed, "seq", split_axis=1, concat_axis=0, tiled=True)
    width = gate_codes.shape[1]
    gate_part = jnp.dot(columns, gate_codes, preferred_element_type=jnp.float32)
    up_part = jnp.dot(columns, up_codes, preferred_element_type=jnp.float32)
    summed = lax.psum_scatter(
        jnp.concatenate([gate_part, up_part], axis=1), "seq", scatter_dimension=0, tiled=True
    )
    gate = summed[:, :width] * gate_scale
    up = summed[:, width:] * up_scale
    activated = (jax.nn.silu(gate) * up).astype(jnp.bfloat16)
    flipped = activated * (1 - 2 * sign_bits).astype(jnp.bfloat16)
    rows_here = flipped.shape[0]
    factor = had52.shape[0]
    local_span = flipped.shape[1] // factor
    shaped = flipped.reshape(rows_here, local_span, factor)
    first = jnp.einsum(
        "rba,ca->rbc", shaped, had52.astype(jnp.bfloat16), preferred_element_type=jnp.float32
    )
    second = jnp.einsum(
        "rba,cb->rca", first, sylvester(local_span), precision=lax.Precision.HIGHEST
    )
    partly = second.reshape(rows_here, local_span * factor)
    position = lax.axis_index("tensor")
    for level in range(lax.axis_size("tensor").bit_length() - 1):
        partner = partner_2(partly, "tensor", level)
        upper_half = jnp.bitwise_and(jnp.right_shift(position, level), 1) == 1
        partly = jnp.where(upper_half, partner - partly, partly + partner)
    rotated = (partly * (1.0 / math.sqrt(FF))).astype(jnp.bfloat16)
    partial_out = jnp.dot(
        lax.all_gather(rotated, "seq", axis=0, tiled=True),
        down_codes,
        preferred_element_type=jnp.float32,
    )
    total_out = lax.psum_scatter(
        partial_out.astype(jnp.bfloat16), "tensor", scatter_dimension=0, tiled=True
    ).astype(jnp.float32)
    return (total_out * down_scale).astype(jnp.bfloat16)


def solution(mesh):
    return jax.shard_map(
        per_device,
        mesh=mesh,
        in_specs=(
            P("seq", None),
            P("seq", "tensor"),
            P("seq", "tensor"),
            P("tensor"),
            P("tensor"),
            P("tensor", "seq"),
            P("seq"),
            P("tensor"),
            P(),
        ),
        out_specs=P("tensor", "seq"),
        check_vma=False,
    )
```

profile of v0, /device:TPU:51, one launch (start us, length us, event | category | flops | bytes accessed | tf_op | source)
XLA Modules:
  0.0 479.2 jit_solution(17787477990087292294)
XLA Ops:
  6.5 0.0 copy-start
  6.5 0.0 reduce-scatter.3.cloned.1.call-start
  6.5 1.7 fusion
  8.2 1.5 fusion.1
  9.7 0.1 copy.26
  9.8 19.3 %all_to_all.19 = bf16[64,16,512]{2,0,1:T(8,128)(2,1)S(1)} all-to-all(bf16[64,16,512]{2,0,1:T(8,128)(2,1)S(1)} %bitcast.23), channel_id=1, replica_groups=mesh['seq'=16,'tensor'=16] {'seq'}, dimensions={1} | all-to-all | bytes 2097152 | tf_op jit(solution)/shard_map/all_to_all | solution.py:31
  29.1 0.0 copy-done
  29.1 0.0 copy-start.7
  29.1 3.7 fusion.34
  32.8 0.0 copy-done.7
  32.8 3.7 fusion.35
  36.5 9.5 %pad_maximum_fusion = f32[1024,6656]{1,0:T(8,128)} fusion(f32[1024,3328]{1,0:T(8,128)S(1)} %fusion.35, f32[1024,3328]{1,0:T(8,128)S(1)} %fusion.34), kind=kLoop, calls=%fused_computation | loop fusion | flops 6815744 | bytes 54525952 | tf_op jit(solution)/shard_map/concatenate | solution.py:36
  46.1 0.0 reduce-scatter.3.cloned.1.call-update
  46.1 0.0 copy-start.2
  46.1 0.2 all-gather.2.cloned.1.call-start
  46.3 0.4 copy-done.5
  46.8 170.3 %reduce-scatter.3.cloned.1.call-done = f32[64,6656]{1,0:T(8,128)} async-done(((f32[1024,6656]{1,0:T(8,128)}), f32[64,6656]{1,0:T(8,128)}) %reduce-scatter.3.cloned.1.call-update) | async-done | bytes 1703952 | tf_op jit(solution)/shard_map/reduce_scatter | solution.py:35
  217.1 0.0 copy-done.3
  217.1 0.0 copy-done.4
  217.1 1.7 fusion.9
  218.8 3.1 reshape.21
  222.0 0.0 copy-done.2
  222.0 1.1 fusion.25
  223.1 6.2 %fusion.4 = f32[64,64,52]{0,1,2:T(8,128)} fusion(f32[64,64,52]{1,2,0:T(8,128)S(1)} %fusion.25), kind=kOutput, calls=%fused_computation.7 | convolution fusion | flops 163708928 | bytes 1703936 | tf_op jit(solution)/shard_map/rba,cb->rca/dot_general | solution.py:49
  229.3 3.2 copy.18
  232.5 1.6 reshape.22
  234.2 0.7 collective-permute-start
  234.9 2.0 collective-permute-done
  236.9 0.1 add_select_fusion.2
  237.0 0.3 collective-permute-start.1
  237.2 20.0 %collective-permute-done.1 = f32[64,3328]{1,0:T(8,128)S(1)} collective-permute-done((f32[64,3328]{1,0:T(8,128)S(1)}, f32[64,3328]{1,0:T(8,128)S(1)}, u32[]{:S(2)}, u32[]{:S(2)}) %collective-permute-start.1) | collective-permute-done | bytes 852000 | tf_op jit(solution)/shard_map/ppermute | solution.py:12
  257.2 0.1 add_select_fusion.1
  257.3 2.3 collective-permute-start.2
  259.7 36.8 %collective-permute-done.2 = f32[64,3328]{1,0:T(8,128)S(1)} collective-permute-done((f32[64,3328]{1,0:T(8,128)S(1)}, f32[64,3328]{1,0:T(8,128)S(1)}, u32[]{:S(2)}, u32[]{:S(2)}) %collective-permute-start.2) | collective-permute-done | bytes 852000 | tf_op jit(solution)/shard_map/ppermute | solution.py:12
  296.5 0.1 add_select_fusion
  296.6 2.0 collective-permute-start.3
  298.6 23.2 %collective-permute-done.3 = f32[64,3328]{1,0:T(8,128)S(1)} collective-permute-done((f32[64,3328]{1,0:T(8,128)S(1)}, f32[64,3328]{1,0:T(8,128)S(1)}, u32[]{:S(2)}, u32[]{:S(2)}) %collective-permute-start.3) | collective-permute-done | bytes 852000 | tf_op jit(solution)/shard_map/ppermute | solution.py:12
  321.8 0.9 multiply_convert_fusion
  322.7 0.0 all-gather.2.cloned.1.call-update
  322.7 0.0 copy-start.6
  322.7 0.0 reduce-scatter.5.cloned.1.call-start
  322.8 84.7 %all-gather.2.cloned.1.call-done = bf16[1024,3328]{1,0:T(8,128)(2,1)} async-done(((bf16[64,3328]{1,0:T(8,128)(2,1)}), bf16[1024,3328]{1,0:T(8,128)(2,1)}) %all-gather.2.cloned.1.call-update) | async-done | bytes 6815760 | tf_op jit(solution)/shard_map/all_gather | solution.py:60
  407.4 8.7 %convolution_convert_fusion = bf16[1024,512]{1,0:T(8,128)(2,1)} fusion(bf16[1024,3328]{1,0:T(8,128)(2,1)} %all-gather.2.cloned.1.call-done, bf16[3328,512]{1,0:T(8,128)(2,1)} %param.14), kind=kOutput, calls=%fused_computation.8 | convolution fusion | flops 3490185216 | bytes 11272192 | tf_op jit(solution)/shard_map/dot_general | solution.py:59
  416.1 0.0 reduce-scatter.5.cloned.1.call-update
  416.2 55.1 %reduce-scatter.5.cloned.1.call-done = bf16[64,512]{1,0:T(8,128)(2,1)} async-done(((bf16[1024,512]{1,0:T(8,128)(2,1)}), bf16[64,512]{1,0:T(8,128)(2,1)}) %reduce-scatter.5.cloned.1.call-update) | async-done | bytes 65552 | tf_op jit(solution)/shard_map/reduce_scatter | solution.py:64
  471.2 0.0 copy-done.6
  471.2 1.5 multiply_convert_fusion.1
  472.7 0.0 copy-done.1
  (6 shorter events, 0.0 us)
Async XLA Ops:
  6.5 22.6 %copy-start = (bf16[512,3328]{1,0:T(8,128)(2,1)S(1)}, bf16[512,3328]{1,0:T(8,128)(2,1)}, u32[]{:S(2)}) copy-start(bf16[512,3328]{1,0:T(8,128)(2,1)} %param.10) | copy-start | bytes 10223620
  6.5 210.6 %reduce-scatter.3.cloned.1.call-start = ((), (), s32[]{:S(2)}) async-start(), calls=%async_computation.3 | async-start | bytes 28966912 | tf_op jit(solution)/shard_map/reduce_scatter | solution.py:35
  29.1 3.7 copy-start.7
  46.0 0.7 copy-start.5
  46.0 171.1 %copy-start.3 = (f32[3328]{0:T(1024)S(1)}, f32[3328]{0:T(1024)}, u32[]{:S(2)}) copy-start(f32[3328]{0:T(1024)} %param.13) | copy-start | bytes 39940
  46.0 171.1 %copy-start.4 = (f32[3328]{0:T(1024)S(1)}, f32[3328]{0:T(1024)}, u32[]{:S(2)}) copy-start(f32[3328]{0:T(1024)} %param.12) | copy-start | bytes 39940
  46.1 175.9 %copy-start.2 = (s32[52,52]{1,0:T(8,128)S(1)}, s32[52,52]{1,0:T(8,128)}, u32[]{:S(2)}) copy-start(s32[52,52]{1,0:T(8,128)} %param.17) | copy-start | bytes 32452
  46.1 361.3 %all-gather.2.cloned.1.call-start = ((), (), s32[]{:S(2)}) async-start(), calls=%async_computation.4 | async-start | bytes 7241728 | tf_op jit(solution)/shard_map/all_gather | solution.py:60
  234.2 2.7 collective-permute-start
  237.0 20.2 %collective-permute-start.1 = (f32[64,3328]{1,0:T(8,128)S(1)}, f32[64,3328]{1,0:T(8,128)S(1)}, u32[]{:S(2)}, u32[]{:S(2)}) collective-permute-start(f32[64,3328]{1,0:T(8,128)S(1)} %add_select_fusion.2), channel_id=1, source_target_pairs={{0,2},{1,3},{2,0},{3,1},{4,6},{5,7},{6,4},{7,5},{8,10},{9,11},{10,... | collective-permute-start | bytes 2555912 | tf_op jit(solution)/shard_map/ppermute | solution.py:12
  257.3 39.2 %collective-permute-start.2 = (f32[64,3328]{1,0:T(8,128)S(1)}, f32[64,3328]{1,0:T(8,128)S(1)}, u32[]{:S(2)}, u32[]{:S(2)}) collective-permute-start(f32[64,3328]{1,0:T(8,128)S(1)} %add_select_fusion.1), channel_id=1, source_target_pairs={{0,4},{1,5},{2,6},{3,7},{4,0},{5,1},{6,2},{7,3},{8,12},{9,13},{10,... | collective-permute-start | bytes 2555912 | tf_op jit(solution)/shard_map/ppermute | solution.py:12
  296.6 25.2 %collective-permute-start.3 = (f32[64,3328]{1,0:T(8,128)S(1)}, f32[64,3328]{1,0:T(8,128)S(1)}, u32[]{:S(2)}, u32[]{:S(2)}) collective-permute-start(f32[64,3328]{1,0:T(8,128)S(1)} %add_select_fusion), channel_id=1, source_target_pairs={{0,8},{1,9},{2,10},{3,11},{4,12},{5,13},{6,14},{7,15},{8,0},{9,1},... | collective-permute-start | bytes 2555912 | tf_op jit(solution)/shard_map/ppermute | solution.py:12
  322.7 148.5 %copy-start.6 = (f32[512]{0:T(512)S(1)}, f32[512]{0:T(512)}, u32[]{:S(2)}) copy-start(f32[512]{0:T(512)} %param.15) | copy-start | bytes 6148
  322.7 148.5 %reduce-scatter.5.cloned.1.call-start = ((), (), s32[]{:S(2)}) async-start(), calls=%async_computation.5 | async-start | bytes 1114112 | tf_op jit(solution)/shard_map/reduce_scatter | solution.py:64
  407.4 65.3 %copy-start.1 = (bf16[512,3328]{1,0:T(8,128)(2,1)S(1)}, bf16[512,3328]{1,0:T(8,128)(2,1)}, u32[]{:S(2)}) copy-start(bf16[512,3328]{1,0:T(8,128)(2,1)} %param.10) | copy-start | bytes 10223620
Sparse Core Ops, SparseCore 0:
  46.2 170.8 reduce-scatter.2
  322.8 84.5 all-gather.1
  416.3 54.8 reduce-scatter.4
where the time goes:
time: 483 us; the launch traced here: 479 us
  waiting for transfers between devices  392 us (81%)
  matrix products  23.4 us (5%)
  blocking collectives  19.3 us (4%)
  other arithmetic  17 us (4%)
  between operations  13.2 us (3%)
  local copies, waits for them, and re-layouts  8.56 us (2%)
  starting transfers between devices  5.64 us (1%)
    reduce_scatter x1, waiting for transfers between devices, per_device(): lax.psum_scatter(jnp.concatenate([gate_part, up_part], axis=1), 'seq', sc...  170 us
    all_gather x1, waiting for transfers between devices, per_device(): lax.all_gather(rotated, 'seq', axis=0, tiled=True)  84.7 us
    ppermute x4, waiting for transfers between devices, partner_2(): lax.ppermute(shard, axis, [(i, i ^ 1 << distance) for i in range(lax.axis...  82 us
    reduce_scatter x1, waiting for transfers between devices, per_device(): lax.psum_scatter(partial_out.astype(jnp.bfloat16), 'tensor', scatter_dime...  55.1 us
    all_to_all x1, blocking collectives, per_device(): lax.all_to_all(normed, 'seq', split_axis=1, concat_axis=0, tiled=True)  19.3 us
  transfers between devices with their start and end apart: 7, of which 7 were waited for; matrix products, arithmetic and copies ran while one was open for 0% of the time, Pallas kernels for 0%

commit v1 on v0

v1 whole, which is shorter than its diff:
```python
import functools
import math

import jax
import jax.numpy as jnp
import ml_dtypes
import numpy as np
from jax import lax
from jax.experimental import pallas as pl
from jax.experimental.pallas import tpu as pltpu
from jax.sharding import PartitionSpec as P

FF = 53248
SIDE = 4
MESH = pl.DeviceIdType.MESH
F32 = jnp.float32
BF16 = jnp.bfloat16


def mod(value, by):
    return lax.rem(value, by)


def kernel(
    hid_hbm, gate_hbm, up_hbm, gate_scale, up_scale, down_hbm, down_scale, signs, had,
    pick, pick_t, spread, spread_t,
    out_ref,
    hid, x, w, wd, rot, ring, ring2, fin, inv, z1s, z1r, z2s, z2r, ag, outs, outr,
    load_sem, xs, xr, core_sem, r1s, r1r, r2s, r2r, z1ss, z1rs, z2ss, z2rs, ags, agr, os, orr,
):
    seq = lax.axis_index("seq")
    ten = lax.axis_index("tensor")
    n_seq = SIDE * SIDE
    tokens, features = hid.shape
    depth = features // n_seq
    half_rows = tokens // 2
    n_ten = z1r.shape[0]
    groups = n_ten // 2
    width = ring.shape[-1]
    core = mod(ten, 2)
    zed = lax.div(ten, 2)
    other = zed * 2 + 1 - core
    step_a = 1 + (SIDE - 1) * core
    step_b = SIDE - (SIDE - 1) * core
    pos_x, pos_y = mod(seq, SIDE), lax.div(seq, SIDE)
    pa = pos_x * (1 - core) + pos_y * core
    pb = pos_y * (1 - core) + pos_x * core

    def at(a, b):
        return mod(a + 2 * SIDE, SIDE) * step_a + mod(b + 2 * SIDE, SIDE) * step_b

    def remote(src, dst, send, recv, device):
        return pltpu.make_async_remote_copy(
            src_ref=src, dst_ref=dst, send_sem=send, recv_sem=recv, device_id=device, device_id_type=MESH
        )

    loads = [pltpu.make_async_copy(hid_hbm, hid, load_sem.at[0])]
    for j, (source, part) in enumerate(((gate_hbm, 0), (gate_hbm, 1), (up_hbm, 0), (up_hbm, 1))):
        loads.append(
            pltpu.make_async_copy(source.at[:, part * width : (part + 1) * width], w.at[j], load_sem.at[1 + j])
        )
    for h in range(2):
        loads.append(
            pltpu.make_async_copy(down_hbm.at[h * width : (h + 1) * width, :], wd.at[h], load_sem.at[5 + h])
        )
    for load in loads:
        load.start()

    barrier = pltpu.get_barrier_semaphore()

    def greet_seq(d, c):
        pl.semaphore_signal(barrier, inc=1, device_id={"seq": mod(seq + d, n_seq)}, device_id_type=MESH)
        return c

    def greet_ten(d, c):
        pl.semaphore_signal(barrier, inc=1, device_id={"tensor": mod(ten + d, n_ten)}, device_id_type=MESH)
        return c

    lax.fori_loop(1, n_seq, greet_seq, 0)
    lax.fori_loop(1, n_ten, greet_ten, 0)
    pl.semaphore_wait(barrier, n_seq + n_ten - 2)

    my_rows = pl.ds(pl.multiple_of(core * half_rows, half_rows), half_rows)

    def piece(d):
        peer = mod(seq + d, n_seq)
        return remote(
            hid_hbm.at[my_rows, pl.ds(pl.multiple_of(peer * depth, depth), depth)],
            x.at[core, seq],
            xs.at[d],
            xr.at[d],
            {"seq": peer},
        )

    def send_piece(d, c):
        piece(d).start()
        return c

    lax.fori_loop(1, n_seq, send_piece, 0)
    own = pltpu.make_async_copy(
        hid_hbm.at[my_rows, pl.ds(pl.multiple_of(seq * depth, depth), depth)], x.at[core, seq], xs.at[0]
    )
    own.start()

    rows_at_once = 128

    def build(r, c):
        rows = pl.ds(pl.multiple_of(r * rows_at_once, rows_at_once), rows_at_once)
        mixed = lax.dot_general(
            pick[rows, :], had[...].astype(F32).astype(BF16), (((1,), (1,)), ((), ())), preferred_element_type=F32
        )
        small = jnp.dot(mixed.astype(BF16), pick_t[...], preferred_element_type=F32)
        large = jnp.dot(spread[rows, :], spread_t[...], preferred_element_type=F32)
        rot[rows, :] = (small * large).astype(BF16)
        return c

    lax.fori_loop(0, width // rows_at_once, build, 0)
    loads[0].wait()
    chunk = min(1024, features)

    def squares(i, total):
        part = hid[:, pl.ds(pl.multiple_of(i * chunk, chunk), chunk)].astype(F32)
        return total + jnp.sum(part * part, axis=1, keepdims=True)

    total = lax.fori_loop(0, features // chunk, squares, jnp.zeros((tokens, 1), F32))
    inv[...] = jnp.broadcast_to(lax.rsqrt(total * (1.0 / features) + 1e-05), inv.shape)

    own.wait()

    def got_piece(d, c):
        piece(d).wait_recv()
        return c

    lax.fori_loop(1, n_seq, got_piece, 0)
    swap = remote(x.at[core], x.at[core], core_sem.at[0], core_sem.at[1], {"tensor": other})
    swap.start()
    for load in loads[1:5]:
        load.wait()
    swap.wait()

    def block_of(stream, step):
        return 3 - step if stream == 0 else 1 + step

    ahead = (1, SIDE - 1)

    def product(stream, step, j):
        a = pa + block_of(stream, step)
        rows = jnp.concatenate([x[stream, at(a, b)] for b in range(SIDE)], axis=0)
        return jnp.dot(rows, w[j], preferred_element_type=F32).reshape(SIDE, half_rows, width)

    def ring_copy(stream, step, j):
        return remote(
            ring.at[step, stream, j],
            ring.at[step + 1, stream, j],
            r1s.at[step, stream, j],
            r1r.at[step, stream, j],
            {"seq": at(pa + ahead[stream], pb)},
        )

    def ring2_copy(stream, step, j):
        if isinstance(step, int) and step == 0:
            source = ring.at[3, stream, j, mod(pb + block_of(stream, 0), SIDE)]
        else:
            source = ring2.at[step - 1, stream, j]
        return remote(
            source,
            ring2.at[step, stream, j],
            r2s.at[step, stream, j],
            r2r.at[step, stream, j],
            {"seq": at(pa, pb + ahead[stream])},
        )

    def first_step(j, c):
        for stream in range(2):
            ring[0, stream, j] = product(stream, 0, j).astype(BF16)
            ring_copy(stream, 0, j).start()
        return c

    lax.fori_loop(0, 4, first_step, 0)

    def next_step(i, c):
        step, j = 1 + lax.div(i, 4), mod(i, 4)
        for stream in range(2):
            value = product(stream, step, j)
            ring_copy(stream, step - 1, j).wait_recv()
            ring[step, stream, j] = (value + ring[step, stream, j].astype(F32)).astype(BF16)
            ring_copy(stream, step, j).start()
        return c

    lax.fori_loop(0, 8, next_step, 0)

    def last_steps(n, c):
        @pl.when(n < 4)
        def _():
            for stream in range(2):
                value = product(stream, 3, n)
                ring_copy(stream, 2, n).wait_recv()
                ring[3, stream, n] = (value + ring[3, stream, n].astype(F32)).astype(BF16)
                ring2_copy(stream, 0, n).start()

        for step in (1, 2, 3):

            @pl.when(jnp.logical_and(n >= step, n < 4 + step))
            def _():
                j = n - step
                for stream in range(2):
                    ring2_copy(stream, step - 1, j).wait_recv()
                    block = mod(pb + block_of(stream, step), SIDE)
                    value = ring[3, stream, j, block].astype(F32) + ring2[step - 1, stream, j].astype(F32)
                    if step < 3:
                        ring2[step - 1, stream, j] = value.astype(BF16)
                        ring2_copy(stream, step, j).start()
                    else:
                        fin[stream, j] = value

        return c

    lax.fori_loop(0, 7, last_steps, 0)

    for stream in range(2):
        rows = slice(stream * half_rows, (stream + 1) * half_rows)
        scale = inv[rows, 0:1]
        acts = []
        for h in range(2):
            cols = slice(h * width, (h + 1) * width)
            gate = fin[stream, h] * scale * gate_scale[:, cols]
            up = fin[stream, 2 + h] * scale * up_scale[:, cols]
            act = gate / (1.0 + jnp.exp(-gate)) * up
            acts.append(act * (1 - 2 * signs[:, cols]).astype(F32))
        in_group = tokens // groups
        per_stream = groups // 2
        for h, value in enumerate((acts[0] + acts[1], acts[0] - acts[1])):
            z1s[h, stream * per_stream : (stream + 1) * per_stream] = value.reshape(
                per_stream, in_group, width
            ).astype(BF16)

    def out_copy(d):
        peer = mod(ten + d, n_ten)
        return remote(
            z1s.at[mod(peer, 2), lax.div(peer, 2)], z1r.at[ten], z1ss.at[d], z1rs.at[d], {"tensor": peer}
        )

    def back_copy(d):
        peer = mod(ten + d, n_ten)
        return remote(z2s.at[peer], z2r.at[core, zed], z2ss.at[d], z2rs.at[d], {"tensor": peer})

    def start_of(copy):
        def go(d, c):
            copy(d).start()
            return c

        return go

    def arrival_of(copy):
        def go(d, c):
            copy(d).wait_recv()
            return c

        return go

    def departure_of(copy):
        def go(d, c):
            copy(d).wait_send()
            return c

        return go

    lax.fori_loop(1, n_ten, start_of(out_copy), 0)
    z1r[ten] = z1s[core, zed]
    lax.fori_loop(1, n_ten, arrival_of(out_copy), 0)
    spun = jnp.dot(
        z1r[...].astype(F32).reshape(n_ten * in_group, width).astype(BF16), rot[...], preferred_element_type=F32
    )
    spun = spun * (1.0 / math.sqrt(FF))
    span = 1
    while span < n_ten:
        pairs = spun.reshape(n_ten // (2 * span), 2, span * in_group, width)
        low, high = pairs[:, 0:1], pairs[:, 1:2]
        spun = jnp.concatenate([low + high, low - high], axis=1)
        span *= 2
    z2s[...] = spun.reshape(n_ten, in_group, width).astype(BF16)
    lax.fori_loop(1, n_ten, start_of(back_copy), 0)
    z2r[core, zed] = z2s[ten]
    lax.fori_loop(1, n_ten, arrival_of(back_copy), 0)
    for h in range(2):
        ag[seq, h] = z2r[h].astype(F32).reshape(tokens, width).astype(BF16)

    count = iter(range(30))
    pending = []

    def pass_on(s, h, target):
        n = next(count)
        copy = remote(ag.at[s, h], ag.at[s, h], ags.at[n], agr.at[s, h], {"seq": target})
        copy.start()
        pending.append(copy)

    def arrived(s, h):
        remote(ag.at[s, h], ag.at[s, h], ags.at[0], agr.at[s, h], {"seq": seq}).wait_recv()

    def send_first(s, a_step, b_step):
        for h0, h1 in ((0, 1), (1, 0)):
            pass_on(s, h0, at(pa + a_step, pb + b_step))
            pass_on(s, h1, at(pa - a_step, pb - b_step))

    def multiply(blocks):
        total = None
        for h in range(2):
            rows = jnp.concatenate([ag[s, h] for s in blocks], axis=0)
            part = jnp.dot(rows, wd[h], preferred_element_type=F32)
            total = part if total is None else total + part
        for i, s in enumerate(blocks):
            outs[s] = total[i * tokens : (i + 1) * tokens].astype(BF16)

            @pl.when(s != ten)
            def _():
                partial(s).start()

            @pl.when(s == ten)
            def _():
                outr[ten] = outs[s]

    def partial(s):
        return remote(outs.at[s], outr.at[ten], os.at[s], orr.at[ten], {"tensor": s})

    for load in loads[5:]:
        load.wait()
    send_first(seq, 1, 0)
    send_first(seq, 0, 1)
    arrived(at(pa, pb - 1), 0)
    pass_on(at(pa, pb - 1), 0, at(pa, pb + 1))
    arrived(at(pa, pb + 1), 1)
    pass_on(at(pa, pb + 1), 1, at(pa, pb - 1))
    arrived(at(pa, pb - 1), 1)
    send_first(at(pa, pb - 1), 1, 0)
    arrived(at(pa, pb + 1), 0)
    send_first(at(pa, pb + 1), 1, 0)

    def forward(b):
        arrived(at(pa - 1, b), 0)
        pass_on(at(pa - 1, b), 0, at(pa + 1, pb))
        arrived(at(pa + 1, b), 1)
        pass_on(at(pa + 1, b), 1, at(pa - 1, pb))

    def near(b):
        arrived(at(pa - 1, b), 1)
        arrived(at(pa + 1, b), 0)
        multiply([at(pa, b), at(pa - 1, b), at(pa + 1, b)])

    def far(b):
        arrived(at(pa + 2, b), 0)
        arrived(at(pa + 2, b), 1)
        multiply([at(pa + 2, b)])

    forward(pb)
    for h in range(2):
        arrived(at(pa, pb + 2), h)
    send_first(at(pa, pb + 2), 1, 0)
    near(pb)
    forward(pb - 1)
    far(pb)
    near(pb - 1)
    forward(pb + 1)
    far(pb - 1)
    near(pb + 1)
    forward(pb + 2)
    far(pb + 1)
    near(pb + 2)
    far(pb + 2)

    def from_tensor(t, c):
        @pl.when(t != ten)
        def _():
            remote(outs.at[t], outr.at[t], os.at[t], orr.at[t], {"tensor": t}).wait()

        return c

    lax.fori_loop(0, n_ten, from_tensor, 0)
    total = outr[0].astype(F32)
    for t in range(1, n_ten):
        total = total + outr[t].astype(F32)
    out_ref[...] = (total * down_scale[...]).astype(out_ref.dtype)

    def piece_left(d, c):
        piece(d).wait_send()
        return c

    lax.fori_loop(1, n_seq, piece_left, 0)

    def rings_left(j, c):
        for step in range(3):
            for stream in range(2):
                ring_copy(stream, step, j).wait_send()
                ring2_copy(stream, step, j).wait_send()
        return c

    lax.fori_loop(0, 4, rings_left, 0)
    lax.fori_loop(1, n_ten, departure_of(out_copy), 0)
    lax.fori_loop(1, n_ten, departure_of(back_copy), 0)
    for copy in pending:
        copy.wait_send()


def sylvester(length):
    matrix = np.ones((1, 1), np.float32)
    while matrix.shape[0] < length:
        matrix = np.kron(np.array([[1, 1], [1, -1]], np.float32), matrix)
    return matrix


def per_device(
    hidden_in, gate_codes, up_codes, gate_scale, up_scale, down_codes, down_scale, sign_bits, had52
):
    tokens, features = hidden_in.shape
    depth, block = gate_codes.shape
    width = block // 2
    factor = had52.shape[0]
    span = width // factor
    columns = down_codes.shape[1]
    n_seq = SIDE * SIDE
    n_ten = lax.axis_size("tensor")
    groups = n_ten // 2
    units = np.arange(width)
    pick = (units[:, None] % factor == np.arange(factor)[None, :]).astype(ml_dtypes.bfloat16)
    own_span = (units[:, None] // factor == np.arange(span)[None, :]).astype(np.float32)
    spread = (own_span @ sylvester(span)).astype(ml_dtypes.bfloat16)
    spread_t = np.ascontiguousarray(own_span.T).astype(ml_dtypes.bfloat16)
    pick_t = np.ascontiguousarray(pick.T)
    vmem = pl.BlockSpec(memory_space=pltpu.VMEM)
    anywhere = pl.BlockSpec(memory_space=pl.ANY)
    dma = pltpu.SemaphoreType.DMA
    small = (n_ten, tokens // groups, width)
    halves = (2, groups, tokens // groups, width)
    return pl.pallas_call(
        kernel,
        out_shape=jax.ShapeDtypeStruct((tokens, columns), BF16),
        in_specs=[anywhere, anywhere, anywhere, vmem, vmem, anywhere, vmem, vmem, vmem] + [vmem] * 4,
        out_specs=vmem,
        scratch_shapes=[
            pltpu.VMEM((tokens, features), BF16),
            pltpu.VMEM((2, n_seq, tokens // 2, depth), BF16),
            pltpu.VMEM((4, depth, width), BF16),
            pltpu.VMEM((2, width, columns), BF16),
            pltpu.VMEM((width, width), BF16),
            pltpu.VMEM((4, 2, 4, SIDE, tokens // 2, width), BF16),
            pltpu.VMEM((3, 2, 4, tokens // 2, width), BF16),
            pltpu.VMEM((2, 4, tokens // 2, width), F32),
            pltpu.VMEM((tokens, 128), F32),
            pltpu.VMEM(halves, BF16),
            pltpu.VMEM(small, BF16),
            pltpu.VMEM(small, BF16),
            pltpu.VMEM(halves, BF16),
            pltpu.VMEM((n_seq, 2, tokens, width), BF16),
            pltpu.VMEM((n_seq, tokens, columns), BF16),
            pltpu.VMEM((n_ten, tokens, columns), BF16),
            dma((7,)),
            dma((n_seq,)),
            dma((n_seq,)),
            dma((2,)),
            dma((3, 2, 4)),
            dma((3, 2, 4)),
            dma((3, 2, 4)),
            dma((3, 2, 4)),
            dma((n_ten,)),
            dma((n_ten,)),
            dma((n_ten,)),
            dma((n_ten,)),
            dma((30,)),
            dma((n_seq, 2)),
            dma((n_seq,)),
            dma((n_ten,)),
        ],
        compiler_params=pltpu.CompilerParams(
            collective_id=0, has_side_effects=True, vmem_limit_bytes=62 * 2**20
        ),
        cost_estimate=pl.CostEstimate(flops=11 * 10**9, bytes_accessed=12 * 10**6, transcendentals=10**6),
    )(
        hidden_in,
        gate_codes,
        up_codes,
        gate_scale.reshape(1, block),
        up_scale.reshape(1, block),
        down_codes,
        down_scale.reshape(1, columns),
        sign_bits.reshape(1, block),
        had52,
        pick,
        pick_t,
        spread,
        spread_t,
    )


def solution(mesh):
    return jax.shard_map(
        per_device,
        mesh=mesh,
        in_specs=(
            P("seq", None),
            P("seq", "tensor"),
            P("seq", "tensor"),
            P("tensor"),
            P("tensor"),
            P("tensor", "seq"),
            P("seq"),
            P("tensor"),
            P(),
        ),
        out_specs=P("tensor", "seq"),
        check_vma=False,
    )
```

time: 483 us -> 184 us (0.38)
  waiting for transfers between devices: 392 us -> 0 us
  Pallas kernels: 0 us -> 178 us
  matrix products: 23.4 us -> 0 us
  blocking collectives: 19.3 us -> 0 us
  other arithmetic: 17 us -> 0 us
  between operations: 13.2 us -> 0.01 us
  starting transfers between devices: 5.64 us -> 0 us
    reduce_scatter x2 -> x0, waiting for transfers between devices: 225 us -> none  [the longest x1 170 us: per_device(): lax.psum_scatter(jnp.concatenate([gate_part, up_part], axis=1), 'seq', sc...]
    pallas_call x0 -> x1, Pallas kernels: none -> 178 us  [per_device(): pl.pallas_call(kernel, out_shape=jax.ShapeDtypeStruct((tokens, columns),...]
    all_gather x1 -> x0, waiting for transfers between devices: 84.7 us -> none  [per_device(): lax.all_gather(rotated, 'seq', axis=0, tiled=True)]
    ppermute x4 -> x0, waiting for transfers between devices: 82 us -> none  [partner_2(): lax.ppermute(shard, axis, [(i, i ^ 1 << distance) for i in range(lax.axis...]
    dot_general x5 -> x0, matrix products: 23.4 us -> none  [the longest x1 8.7 us: per_device(): jnp.dot(lax.all_gather(rotated, 'seq', axis=0, tiled=True), down_codes, p...]
    all_to_all x1 -> x0, blocking collectives: 19.3 us -> none  [per_device(): lax.all_to_all(normed, 'seq', split_axis=1, concat_axis=0, tiled=True)]
    concatenate x1 -> x0, other arithmetic: 9.52 us -> none  [per_device(): jnp.concatenate([gate_part, up_part], axis=1)]
    ppermute x4 -> x0, starting transfers between devices: 5.38 us -> none  [partner_2(): lax.ppermute(shard, axis, [(i, i ^ 1 << distance) for i in range(lax.axis...]
  transfers between devices with their start and end apart: 7 -> 0, of which waited for: 7 -> 0; matrix products, arithmetic and copies ran while one was open for 0% -> 0% of each run, Pallas kernels for 0% -> 0%
where the time goes in v1:
time: 184 us; the launch traced here: 183 us
  Pallas kernels  178 us (97%)
  local copies, waits for them, and re-layouts  5.45 us (3%)
    pallas_call x1, Pallas kernels, per_device(): pl.pallas_call(kernel, out_shape=jax.ShapeDtypeStruct((tokens, columns),...  178 us

profile of v1, /device:TPU:51, one launch (start us, length us, event | category | flops | bytes accessed | tf_op | source)
XLA Modules:
  0.0 183.1 jit_solution(17307260795836546685)
XLA Ops:
  0.0 1.3 reshape.12.gate_scale
  1.3 1.3 reshape.13.up_scale
  2.6 1.3 reshape.15.signs
  4.0 177.6 %shard_map.127 = bf16[64,512]{1,0:T(8,128)(2,1)} custom-call(bf16[64,8192]{1,0:T(8,128)(2,1)} %hid_hbm.1, bf16[512,3328]{1,0:T(8,128)(2,1)} %gate_hbm.1, bf16[512,3328]{1,0:T(8,128)(2,1)} %up_hbm.1, f32[1,3328]{1,0:T(1,128)} %reshape.12.gate_scale, f32[1,3328]{1,0:T(1,128)} %reshape.13.up_scale, bf16[3328,512]{1,0:T(8,128)(2,1)} %down_hbm.1, ...), custom_call_target="tpu_custom_call" | custom-call | flops 11000000512 | bytes 12000000 | tf_op jit(solution)/shard_map/pallas_call | solution.py:433
  181.6 1.5 copy.15

commit v2 on v1

v2 whole, which is shorter than its diff:
```python
import functools
import math

import jax
import jax.numpy as jnp
import ml_dtypes
import numpy as np
from jax import lax
from jax.experimental import pallas as pl
from jax.experimental.pallas import tpu as pltpu
from jax.sharding import PartitionSpec as P

FF = 53248
SIDE = 4
MESH = pl.DeviceIdType.MESH
F32 = jnp.float32
BF16 = jnp.bfloat16


def mod(value, by):
    return lax.rem(value, by)


def kernel(
    hid_hbm, gate_hbm, up_hbm, gate_scale_hbm, up_scale_hbm, down_hbm, down_scale_hbm, signs_hbm, had_hbm,
    pick_hbm, pick_t_hbm, spread_hbm, spread_t_hbm,
    out_ref,
    gate_scale, up_scale, down_scale, signs, had, pick, pick_t, spread, spread_t, hid, x, w, wd, wx, ring, ring2, fin, inv, z1s, z1r, z2s, z2r, ag, acc, outs, outr,
    load_sem, xs, xr, core_sem, r1s, r1r, r2s, r2r, z1ss, z1rs, z2ss, z2rs, ags, agr, os, orr,
):
    seq = lax.axis_index("seq")
    ten = lax.axis_index("tensor")
    n_seq = SIDE * SIDE
    tokens, features = hid.shape
    depth = features // n_seq
    half_rows = tokens // 2
    n_ten = outr.shape[0]
    groups = n_ten // 2
    in_group = tokens // groups
    per_stream = groups // 2
    width = ring.shape[-1]
    core = mod(ten, 2)
    zed = lax.div(ten, 2)
    other = zed * 2 + 1 - core
    step_a = 1 + (SIDE - 1) * core
    step_b = SIDE - (SIDE - 1) * core
    pos_x, pos_y = mod(seq, SIDE), lax.div(seq, SIDE)
    pa = pos_x * (1 - core) + pos_y * core
    pb = pos_y * (1 - core) + pos_x * core

    def at(a, b):
        return mod(a + 2 * SIDE, SIDE) * step_a + mod(b + 2 * SIDE, SIDE) * step_b

    def remote(src, dst, send, recv, device):
        return pltpu.make_async_remote_copy(
            src_ref=src, dst_ref=dst, send_sem=send, recv_sem=recv, device_id=device, device_id_type=MESH
        )

    barrier = pltpu.get_barrier_semaphore()

    def greet_seq(d, c):
        pl.semaphore_signal(barrier, inc=1, device_id={"seq": mod(seq + d, n_seq)}, device_id_type=MESH)
        return c

    def greet_ten(d, c):
        pl.semaphore_signal(barrier, inc=1, device_id={"tensor": mod(ten + d, n_ten)}, device_id_type=MESH)
        return c

    lax.fori_loop(1, n_seq, greet_seq, 0)
    lax.fori_loop(1, n_ten, greet_ten, 0)

    loads = [pltpu.make_async_copy(hid_hbm, hid, load_sem.at[0])]
    for j, (source, part) in enumerate(((gate_hbm, 0), (up_hbm, 0), (gate_hbm, 1), (up_hbm, 1))):
        loads.append(
            pltpu.make_async_copy(source.at[:, part * width : (part + 1) * width], w.at[j], load_sem.at[1 + j])
        )
    for h in range(2):
        loads.append(
            pltpu.make_async_copy(down_hbm.at[h * width : (h + 1) * width, :], wd.at[h], load_sem.at[5 + h])
        )
    small = (
        (gate_scale_hbm, gate_scale), (up_scale_hbm, up_scale), (down_scale_hbm, down_scale), (signs_hbm, signs),
        (had_hbm, had), (pick_hbm, pick), (pick_t_hbm, pick_t), (spread_hbm, spread), (spread_t_hbm, spread_t),
    )
    for i, (source, target) in enumerate(small):
        loads.append(pltpu.make_async_copy(source, target, load_sem.at[7 + i]))
    for load in loads:
        load.start()
    pl.semaphore_wait(barrier, n_seq + n_ten - 2)

    my_rows = pl.ds(pl.multiple_of(core * half_rows, half_rows), half_rows)

    def piece(d):
        peer = mod(seq + d, n_seq)
        return remote(
            hid_hbm.at[my_rows, pl.ds(pl.multiple_of(peer * depth, depth), depth)],
            x.at[core, seq],
            xs.at[d],
            xr.at[d],
            {"seq": peer},
        )

    def send_piece(d, c):
        piece(d).start()
        return c

    lax.fori_loop(1, n_seq, send_piece, 0)
    own = pltpu.make_async_copy(
        hid_hbm.at[my_rows, pl.ds(pl.multiple_of(seq * depth, depth), depth)], x.at[core, seq], xs.at[0]
    )
    own.start()

    loads[0].wait()
    chunk = min(1024, features)

    def squares(i, total):
        part = hid[:, pl.ds(pl.multiple_of(i * chunk, chunk), chunk)].astype(F32)
        return total + jnp.sum(part * part, axis=1, keepdims=True)

    total = lax.fori_loop(0, features // chunk, squares, jnp.zeros((tokens, 1), F32))
    inv[...] = jnp.broadcast_to(lax.rsqrt(total * (1.0 / features) + 1e-05), inv.shape)

    own.wait()

    def got_piece(d, c):
        piece(d).wait_recv()
        return c

    lax.fori_loop(1, n_seq, got_piece, 0)
    swap = remote(x.at[core], x.at[core], core_sem.at[0], core_sem.at[1], {"tensor": other})
    swap.start()
    lend = []
    for h in range(2):
        lend.append(
            remote(
                down_hbm.at[h * width : (h + 1) * width, :],
                wx.at[h],
                core_sem.at[2 + 2 * h],
                core_sem.at[3 + 2 * h],
                {"tensor": other},
            )
        )
        lend[h].start()
    for load in loads[1:]:
        load.wait()
    swap.wait()

    def block_of(stream, step):
        return 3 - step if stream == 0 else 1 + step

    ahead = (1, SIDE - 1)

    def product(stream, step, j):
        a = pa + block_of(stream, step)
        rows = jnp.concatenate([x[stream, at(a, b)] for b in range(SIDE)], axis=0)
        return jnp.dot(rows, w[j], preferred_element_type=F32).reshape(SIDE, half_rows, width)

    def ring_copy(stream, step, j):
        return remote(
            ring.at[step, stream, j],
            ring.at[step + 1, stream, j],
            r1s.at[step, stream, j],
            r1r.at[step, stream, j],
            {"seq": at(pa + ahead[stream], pb)},
        )

    def ring2_copy(stream, step, j):
        if step == 0:
            source = ring.at[3, stream, j, mod(pb + block_of(stream, 0), SIDE)]
        else:
            source = ring2.at[step - 1, stream, j]
        return remote(
            source,
            ring2.at[step, stream, j],
            r2s.at[step, stream, j],
            r2r.at[step, stream, j],
            {"seq": at(pa, pb + ahead[stream])},
        )

    def first_axis(h, step):
        def go(j, c):
            for stream in range(2):
                value = product(stream, step, j)
                if step > 0:
                    ring_copy(stream, step - 1, j).wait_recv()
                    value = value + ring[step, stream, j].astype(F32)
                ring[step, stream, j] = value.astype(BF16)
                if step < 3:
                    ring_copy(stream, step, j).start()
                else:
                    ring2_copy(stream, 0, j).start()
            return c

        lax.fori_loop(2 * h, 2 * h + 2, go, 0)

    def second_axis(h, step):
        def go(j, c):
            for stream in range(2):
                ring2_copy(stream, step - 1, j).wait_recv()
                block = mod(pb + block_of(stream, step), SIDE)
                value = ring[3, stream, j, block].astype(F32) + ring2[step - 1, stream, j].astype(F32)
                if step < 3:
                    ring2[step - 1, stream, j] = value.astype(BF16)
                    ring2_copy(stream, step, j).start()
                else:
                    fin[stream, j] = value
            return c

        lax.fori_loop(2 * h, 2 * h + 2, go, 0)

    rows_at_once = 128

    def rows_of(r):
        return pl.ds(pl.multiple_of(r * rows_at_once, rows_at_once), rows_at_once)

    def combine():
        for copy in lend:
            copy.wait()
        sign = (1 - 2 * core).astype(F32)

        def go(r, c):
            rows = rows_of(r)
            d0, d1 = wd[0, rows, :].astype(F32), wd[1, rows, :].astype(F32)
            x0, x1 = wx[0, rows, :].astype(F32), wx[1, rows, :].astype(F32)
            wd[0, rows, :] = (x0 + x1 + sign * (d0 + d1)).astype(BF16)
            wd[1, rows, :] = (x0 - x1 + sign * (d0 - d1)).astype(BF16)
            return c

        lax.fori_loop(0, width // rows_at_once, go, 0)

    def rotate(first, last):
        def go(r, c):
            rows = rows_of(r)
            mixed = lax.dot_general(
                pick[rows, :], had[...].astype(F32).astype(BF16), (((1,), (1,)), ((), ())), preferred_element_type=F32
            )
            small = jnp.dot(mixed.astype(BF16), pick_t[...], preferred_element_type=F32)
            large = jnp.dot(spread[rows, :], spread_t[...], preferred_element_type=F32)
            matrix = (small * large).astype(BF16)
            for h in range(2):
                wx[h, rows, :] = jnp.dot(matrix, wd[h], preferred_element_type=F32).astype(BF16)
            return c

        count = width // rows_at_once
        lax.fori_loop(min(first, count), min(last, count), go, 0)

    def out_copy(h):
        def copy(d):
            peer = mod(zed + d, groups)
            return remote(
                z1s.at[h, peer], z1r.at[h, zed], z1ss.at[h, d], z1rs.at[h, d], {"tensor": peer * 2 + core}
            )

        return copy

    def back_copy(h):
        def copy(d):
            peer = mod(zed + d, groups)
            return remote(
                z2s.at[h, peer], z2r.at[h, zed], z2ss.at[h, d], z2rs.at[h, d], {"tensor": peer * 2 + core}
            )

        return copy

    def start_all(copy):
        def go(d, c):
            copy(d).start()
            return c

        lax.fori_loop(1, groups, go, 0)

    def arrive_all(copy):
        def go(d, c):
            copy(d).wait_recv()
            return c

        lax.fori_loop(1, groups, go, 0)

    def leave_all(copy):
        def go(d, c):
            copy(d).wait_send()
            return c

        lax.fori_loop(1, groups, go, 0)

    def activate(h):
        cols = slice(h * width, (h + 1) * width)
        for stream in range(2):
            rows = slice(stream * half_rows, (stream + 1) * half_rows)
            scale = inv[rows, 0:1]
            gate = fin[stream, 2 * h] * scale * gate_scale[cols].reshape(1, width)
            up = fin[stream, 2 * h + 1] * scale * up_scale[cols].reshape(1, width)
            act = gate / (1.0 + jnp.exp(-gate)) * up
            flipped = act * (1 - 2 * signs[cols].reshape(1, width)).astype(F32)
            z1s[h, stream * per_stream : (stream + 1) * per_stream] = flipped.reshape(
                per_stream, in_group, width
            ).astype(BF16)
        start_all(out_copy(h))
        z1r[h, zed] = z1s[h, zed]

    def mix(h):
        arrive_all(out_copy(h))
        value = z1r[h].astype(F32) * (1.0 / math.sqrt(FF))
        span = 1
        while span < groups:
            pairs = value.reshape(groups // (2 * span), 2, span * in_group, width)
            low, high = pairs[:, 0:1], pairs[:, 1:2]
            value = jnp.concatenate([low + high, low - high], axis=1)
            span *= 2
        z2s[h] = value.reshape(groups, in_group, width).astype(BF16)
        start_all(back_copy(h))
        z2r[h, zed] = z2s[h, zed]

    counts = [iter(range(30)), iter(range(30))]
    pending = []

    def pass_on(h, s, r, target):
        n = next(counts[h])
        copy = remote(ag.at[h, s, r], ag.at[h, s, r], ags.at[h, n], agr.at[h, s, r], {"seq": target})
        copy.start()
        pending.append(copy)

    def arrived(h, s, r):
        remote(ag.at[h, s, r], ag.at[h, s, r], ags.at[h, 0], agr.at[h, s, r], {"seq": seq}).wait_recv()

    def send_first(h, s, a_step, b_step):
        for r0, r1 in ((0, 1), (1, 0)):
            pass_on(h, s, r0, at(pa + a_step, pb + b_step))
            pass_on(h, s, r1, at(pa - a_step, pb - b_step))

    def gather_start(h):
        arrive_all(back_copy(h))
        ag[h, seq] = z2r[h].astype(F32).reshape(2, half_rows, width).astype(BF16)
        send_first(h, seq, 1, 0)
        send_first(h, seq, 0, 1)

    def gather_second(h):
        below, above = at(pa, pb - 1), at(pa, pb + 1)
        arrived(h, below, 0)
        pass_on(h, below, 0, above)
        arrived(h, above, 1)
        pass_on(h, above, 1, below)
        arrived(h, below, 1)
        send_first(h, below, 1, 0)
        arrived(h, above, 0)
        send_first(h, above, 1, 0)

    def gather_opposite(h):
        for r in range(2):
            arrived(h, at(pa, pb + 2), r)
        send_first(h, at(pa, pb + 2), 1, 0)

    def forward(h, b):
        arrived(h, at(pa - 1, b), 0)
        pass_on(h, at(pa - 1, b), 0, at(pa + 1, pb))
        arrived(h, at(pa + 1, b), 1)
        pass_on(h, at(pa + 1, b), 1, at(pa - 1, pb))

    def partial(s):
        return remote(outs.at[s], outr.at[ten], os.at[s], orr.at[ten], {"tensor": s})

    def multiply(h, blocks):
        rows = jnp.concatenate([ag[h, s].reshape(tokens, width) for s in blocks], axis=0)
        total = jnp.dot(rows, wx[h], preferred_element_type=F32)
        for i, s in enumerate(blocks):
            value = total[i * tokens : (i + 1) * tokens]
            if h == 0:
                acc[s] = value
                continue
            outs[s] = (value + acc[s]).astype(BF16)

            @pl.when(s != ten)
            def _():
                partial(s).start()

            @pl.when(s == ten)
            def _():
                outr[ten] = outs[s]

    def near(h, b):
        arrived(h, at(pa - 1, b), 1)
        arrived(h, at(pa + 1, b), 0)
        multiply(h, [at(pa, b), at(pa - 1, b), at(pa + 1, b)])

    def far(h, b):
        arrived(h, at(pa + 2, b), 0)
        arrived(h, at(pa + 2, b), 1)
        multiply(h, [at(pa + 2, b)])

    first_axis(0, 0)
    first_axis(0, 1)
    combine()
    first_axis(0, 2)
    rotate(0, 2)
    first_axis(1, 0)
    rotate(2, 4)
    first_axis(0, 3)
    rotate(4, 6)
    first_axis(1, 1)
    second_axis(0, 1)
    rotate(6, 8)
    second_axis(0, 2)
    first_axis(1, 2)
    second_axis(0, 3)
    activate(0)
    rotate(8, 11)
    first_axis(1, 3)
    mix(0)
    second_axis(1, 1)
    rotate(11, 13)
    second_axis(1, 2)
    gather_start(0)
    second_axis(1, 3)
    activate(1)
    gather_second(0)
    forward(0, pb)
    mix(1)
    gather_opposite(0)
    forward(0, pb - 1)
    forward(0, pb + 1)
    near(0, pb)
    far(0, pb)
    gather_start(1)
    forward(0, pb + 2)
    near(0, pb - 1)
    gather_second(1)
    far(0, pb - 1)
    forward(1, pb)
    near(0, pb + 1)
    gather_opposite(1)
    far(0, pb + 1)
    forward(1, pb - 1)
    near(0, pb + 2)
    far(0, pb + 2)
    near(1, pb)
    forward(1, pb + 1)
    far(1, pb)
    near(1, pb - 1)
    forward(1, pb + 2)
    far(1, pb - 1)
    near(1, pb + 1)
    far(1, pb + 1)
    near(1, pb + 2)
    far(1, pb + 2)

    def from_tensor(t, c):
        @pl.when(t != ten)
        def _():
            remote(outs.at[t], outr.at[t], os.at[t], orr.at[t], {"tensor": t}).wait()

        return c

    lax.fori_loop(0, n_ten, from_tensor, 0)
    total = outr[0].astype(F32)
    for t in range(1, n_ten):
        total = total + outr[t].astype(F32)
    out_ref[...] = (total * down_scale[...].reshape(1, -1)).astype(out_ref.dtype)

    def piece_left(d, c):
        piece(d).wait_send()
        return c

    lax.fori_loop(1, n_seq, piece_left, 0)

    def rings_left(j, c):
        for step in range(3):
            for stream in range(2):
                ring_copy(stream, step, j).wait_send()
                ring2_copy(stream, step, j).wait_send()
        return c

    lax.fori_loop(0, 4, rings_left, 0)
    for h in range(2):
        leave_all(out_copy(h))
        leave_all(back_copy(h))
    for copy in pending:
        copy.wait_send()


def sylvester(length):
    matrix = np.ones((1, 1), np.float32)
    while matrix.shape[0] < length:
        matrix = np.kron(np.array([[1, 1], [1, -1]], np.float32), matrix)
    return matrix


def per_device(
    hidden_in, gate_codes, up_codes, gate_scale, up_scale, down_codes, down_scale, sign_bits, had52
):
    tokens, features = hidden_in.shape
    depth, block = gate_codes.shape
    width = block // 2
    factor = had52.shape[0]
    span = width // factor
    columns = down_codes.shape[1]
    n_seq = SIDE * SIDE
    n_ten = lax.axis_size("tensor")
    groups = n_ten // 2
    units = np.arange(width)
    pick = (units[:, None] % factor == np.arange(factor)[None, :]).astype(ml_dtypes.bfloat16)
    own_span = (units[:, None] // factor == np.arange(span)[None, :]).astype(np.float32)
    spread = (own_span @ sylvester(span)).astype(ml_dtypes.bfloat16)
    spread_t = np.ascontiguousarray(own_span.T).astype(ml_dtypes.bfloat16)
    pick_t = np.ascontiguousarray(pick.T)
    vmem = pl.BlockSpec(memory_space=pltpu.VMEM)
    anywhere = pl.BlockSpec(memory_space=pl.ANY)
    dma = pltpu.SemaphoreType.DMA
    small = (2, groups, tokens // groups, width)
    return pl.pallas_call(
        kernel,
        out_shape=jax.ShapeDtypeStruct((tokens, columns), BF16),
        in_specs=[anywhere] * 13,
        out_specs=vmem,
        scratch_shapes=[
            pltpu.VMEM((block,), F32),
            pltpu.VMEM((block,), F32),
            pltpu.VMEM((columns,), F32),
            pltpu.VMEM((block,), jnp.int32),
            pltpu.VMEM((factor, factor), jnp.int32),
            pltpu.VMEM((width, factor), BF16),
            pltpu.VMEM((factor, width), BF16),
            pltpu.VMEM((width, span), BF16),
            pltpu.VMEM((span, width), BF16),
            pltpu.VMEM((tokens, features), BF16),
            pltpu.VMEM((2, n_seq, tokens // 2, depth), BF16),
            pltpu.VMEM((4, depth, width), BF16),
            pltpu.VMEM((2, width, columns), BF16),
            pltpu.VMEM((2, width, columns), BF16),
            pltpu.VMEM((4, 2, 4, SIDE, tokens // 2, width), BF16),
            pltpu.VMEM((3, 2, 4, tokens // 2, width), BF16),
            pltpu.VMEM((2, 4, tokens // 2, width), F32),
            pltpu.VMEM((tokens, 128), F32),
            pltpu.VMEM(small, BF16),
            pltpu.VMEM(small, BF16),
            pltpu.VMEM(small, BF16),
            pltpu.VMEM(small, BF16),
            pltpu.VMEM((2, n_seq, 2, tokens // 2, width), BF16),
            pltpu.VMEM((n_seq, tokens, columns), F32),
            pltpu.VMEM((n_seq, tokens, columns), BF16),
            pltpu.VMEM((n_ten, tokens, columns), BF16),
            dma((16,)),
            dma((n_seq,)),
            dma((n_seq,)),
            dma((6,)),
            dma((3, 2, 4)),
            dma((3, 2, 4)),
            dma((3, 2, 4)),
            dma((3, 2, 4)),
            dma((2, groups)),
            dma((2, groups)),
            dma((2, groups)),
            dma((2, groups)),
            dma((2, 30)),
            dma((2, n_seq, 2)),
            dma((n_seq,)),
            dma((n_ten,)),
        ],
        compiler_params=pltpu.CompilerParams(
            collective_id=0, has_side_effects=True, vmem_limit_bytes=62 * 2**20
        ),
        cost_estimate=pl.CostEstimate(flops=11 * 10**9, bytes_accessed=12 * 10**6, transcendentals=10**6),
    )(
        hidden_in,
        gate_codes,
        up_codes,
        gate_scale,
        up_scale,
        down_codes,
        down_scale,
        sign_bits,
        had52,
        pick,
        pick_t,
        spread,
        spread_t,
    )


def solution(mesh):
    return jax.shard_map(
        per_device,
        mesh=mesh,
        in_specs=(
            P("seq", None),
            P("seq", "tensor"),
            P("seq", "tensor"),
            P("tensor"),
            P("tensor"),
            P("tensor", "seq"),
            P("seq"),
            P("tensor"),
            P(),
        ),
        out_specs=P("tensor", "seq"),
        check_vma=False,
    )
```

time: 184 us -> 159 us (0.86)
  Pallas kernels: 178 us -> 157 us
  local copies, waits for them, and re-layouts: 5.45 us -> 1.47 us
    pallas_call x1, Pallas kernels: 178 us -> 157 us  [per_device(): pl.pallas_call(kernel, out_shape=jax.ShapeDtypeStruct((tokens, columns),...]
    reshape x3 -> x0, local copies, waits for them, and re-layouts: 3.97 us -> none  [the longest x1 1.33 us: per_device(): gate_scale.reshape(1, block)]
where the time goes in v2:
time: 159 us
  Pallas kernels  157 us (99%)
    pallas_call x1, Pallas kernels, per_device(): pl.pallas_call(kernel, out_shape=jax.ShapeDtypeStruct((tokens, columns),...  157 us

profile of v2, /device:TPU:51, one launch (start us, length us, event | category | flops | bytes accessed | tf_op | source)
XLA Modules:
  0.0 158.8 jit_solution(7414915902579172734)
XLA Ops:
  0.0 157.4 %shard_map.127 = bf16[64,512]{1,0:T(8,128)(2,1)} custom-call(bf16[64,8192]{1,0:T(8,128)(2,1)} %hid_hbm.1, bf16[512,3328]{1,0:T(8,128)(2,1)} %gate_hbm.1, bf16[512,3328]{1,0:T(8,128)(2,1)} %up_hbm.1, f32[3328]{0:T(1024)} %gate_scale_hbm.1, f32[3328]{0:T(1024)} %up_scale_hbm.1, bf16[3328,512]{1,0:T(8,128)(2,1)} %down_hbm.1, f32[512]{0:T(512)} %down_scale_hbm.1, ...), custom_call_target="tpu_custom_call" | custom-call | flops 11000000512 | bytes 12000000 | tf_op jit(solution)/shard_map/pallas_call | solution.py:509
  157.4 1.5 copy.15

commit v3 on v2

--- a/solution.py
+++ b/solution.py
@@ -84,8 +84,6 @@
     )
     for i, (source, target) in enumerate(small):
         loads.append(pltpu.make_async_copy(source, target, load_sem.at[7 + i]))
-    for load in loads:
-        load.start()
     pl.semaphore_wait(barrier, n_seq + n_ten - 2)
 
     my_rows = pl.ds(pl.multiple_of(core * half_rows, half_rows), half_rows)
@@ -109,6 +107,8 @@
         hid_hbm.at[my_rows, pl.ds(pl.multiple_of(seq * depth, depth), depth)], x.at[core, seq], xs.at[0]
     )
     own.start()
+    for load in loads:
+        load.start()
 
     loads[0].wait()
     chunk = min(1024, features)

time: 159 us -> 159 us (level)
  no operation moved by 1% of the time
where the time goes in v3:
time: 159 us
  Pallas kernels  157 us (99%)
    pallas_call x1, Pallas kernels, per_device(): pl.pallas_call(kernel, out_shape=jax.ShapeDtypeStruct((tokens, columns),...  157 us

profile of v3, /device:TPU:51, one launch (start us, length us, event | category | flops | bytes accessed | tf_op | source)
XLA Modules:
  0.0 158.9 jit_solution(6387149010242340888)
XLA Ops:
  0.0 157.4 %shard_map.127 = bf16[64,512]{1,0:T(8,128)(2,1)} custom-call(bf16[64,8192]{1,0:T(8,128)(2,1)} %hid_hbm.1, bf16[512,3328]{1,0:T(8,128)(2,1)} %gate_hbm.1, bf16[512,3328]{1,0:T(8,128)(2,1)} %up_hbm.1, f32[3328]{0:T(1024)} %gate_scale_hbm.1, f32[3328]{0:T(1024)} %up_scale_hbm.1, bf16[3328,512]{1,0:T(8,128)(2,1)} %down_hbm.1, f32[512]{0:T(512)} %down_scale_hbm.1, ...), custom_call_target="tpu_custom_call" | custom-call | flops 11000000512 | bytes 12000000 | tf_op jit(solution)/shard_map/pallas_call | solution.py:509
  157.4 1.5 copy.15
